TPU v7x, 32 devices: a whole 2x2x4 slice. The times are simulated.
32 devices in a mesh: branch: 2 (over core), row: 2 (over x), col: 8 (over z, y).
Axes of the slice: x: 2, y: 2, z: 4, core: 2. Of those that a mesh axis runs over, the one named last changes fastest.
Arguments:
- tokens: bfloat16 [2, 32, 256, 1152], P('branch', 'row', 'col'), may hold values from -26 to 26
- modulation: float32 [3, 1152], replicated, may hold values from -4 to 4
- wqkv: bfloat16 [1152, 3456], replicated, may hold values from -1 to 1
- w_out: bfloat16 [1152, 1152], replicated, may hold values from -0.1875 to 0.1875
- blend: float32 [32, 256], P('row', 'col'), may hold values from 0.1 to 0.6
- reach: int32 [4, 2, 8], P(None, 'row', 'col'), may hold values from 1 to 4, as said below
Outputs:
- guided: bfloat16 [32, 256, 1152], P(('row', 'branch'), 'col')
Inputs may be any that keep to these rules, and one draw needn't show every extreme that they name: Each reach is at most 4, and some tile's reach on some side is exactly 4.
All inputs are finite; a program needn't handle non-finite values.
Results may differ from a plain program's by a relative error of at most 0.0067.
Values may be sent and summed in bfloat16 or wider, within the bound.
A program may use at most 192 MiB of HBM per device.

v0:
```python
import math

import jax
import jax.numpy as jnp
from jax import lax
from jax.sharding import PartitionSpec as P

HEADS = 16
HALO = 4


GUIDANCE = 4.5


def with_halo(cells, sides, width):
    for axis, dim in sides:
        count = lax.axis_size(axis)
        ends = count - 1
        head = lax.slice_in_dim(cells, 0, width, axis=dim)
        tail = lax.slice_in_dim(cells, cells.shape[dim] - width, cells.shape[dim], axis=dim)
        cells = jnp.concatenate(
            [
                lax.ppermute(tail, axis, [(i, (i + 1) % count) for i in range(ends)]),
                cells,
                lax.ppermute(head, axis, [((i + 1) % count, i) for i in range(ends)]),
            ],
            axis=dim,
        )
    return cells


def layer_norm(values, modulation):
    widened = values.astype(jnp.float32)
    centered = widened - jnp.mean(widened, axis=-1, keepdims=True)
    variance = jnp.mean(centered * centered, axis=-1, keepdims=True)
    scaled = centered * lax.rsqrt(variance + 1e-06)
    return (scaled * (1.0 + modulation[1]) + modulation[0]).astype(jnp.bfloat16)


def project(normed, wqkv):
    feature_width = normed.shape[-1]
    joined = jnp.dot(normed, wqkv, preferred_element_type=jnp.float32).astype(jnp.bfloat16)
    return (
        joined[:, :feature_width],
        joined[:, feature_width : 2 * feature_width],
        joined[:, 2 * feature_width :],
    )


def attend(queries, keys, values, allowed):
    query_count, feature_width = queries.shape
    key_count = keys.shape[0]
    head_size = feature_width // HEADS
    query_heads = queries.reshape(query_count, HEADS, head_size)
    key_heads = keys.reshape(key_count, HEADS, head_size)
    value_heads = values.reshape(key_count, HEADS, head_size)
    scores = jnp.einsum(
        "qhd,khd->hqk", query_heads, key_heads, preferred_element_type=jnp.float32
    ) * (1.0 / math.sqrt(head_size))
    if allowed is not None:
        scores = jnp.where(allowed[None, None, :], scores, -1e30)
    row_max = jnp.max(scores, axis=-1, keepdims=True)
    powers = jnp.exp(scores - row_max)
    weights = (powers / jnp.sum(powers, axis=-1, keepdims=True)).astype(jnp.bfloat16)
    attended = jnp.einsum("hqk,khd->qhd", weights, value_heads, preferred_element_type=jnp.float32)
    return attended.reshape(query_count, feature_width)


def window_mask(reach, rows, cols):
    row_start = lax.axis_index("row") * rows
    col_start = lax.axis_index("col") * cols
    height = rows * lax.axis_size("row")
    breadth = cols * lax.axis_size("col")
    row_offsets = jnp.arange(rows + 2 * HALO, dtype=jnp.int32)
    col_offsets = jnp.arange(cols + 2 * HALO, dtype=jnp.int32)
    global_rows = row_start - HALO + row_offsets
    global_cols = col_start - HALO + col_offsets
    row_fine = (global_rows >= 0) & (global_rows < height)
    row_fine = (
        row_fine
        & (row_offsets >= HALO - reach[0, 0, 0])
        & (row_offsets < HALO + rows + reach[1, 0, 0])
    )
    col_fine = (global_cols >= 0) & (global_cols < breadth)
    col_fine = (
        col_fine
        & (col_offsets >= HALO - reach[2, 0, 0])
        & (col_offsets < HALO + cols + reach[3, 0, 0])
    )
    return (row_fine[:, None] & col_fine[None, :]).reshape(-1)


def on_device(tokens, modulation, wqkv, w_out, blend, reach):
    rows, cols, feature_width = (tokens.shape[1], tokens.shape[2], tokens.shape[3])
    row_groups = lax.axis_size("row")
    col_groups = lax.axis_size("col")
    sub_rows = rows // row_groups
    sub_cols = cols // col_groups
    normed = layer_norm(tokens[0], modulation).reshape(rows * cols, feature_width)
    queries, keys, values = project(normed, wqkv)
    stacked = jnp.stack(
        (keys.reshape(rows, cols, feature_width), values.reshape(rows, cols, feature_width)), axis=0
    )
    window = with_halo(stacked, (("row", 1), ("col", 2)), HALO)
    allowed = window_mask(reach, rows, cols)
    window_out = attend(
        queries, window[0].reshape(-1, feature_width), window[1].reshape(-1, feature_width), allowed
    )
    split = jnp.stack((queries, keys, values), axis=0).reshape(
        -1, sub_rows, row_groups, sub_cols, col_groups, feature_width
    )
    outgoing = split.transpose(0, 2, 4, 1, 3, 5).reshape(
        -1, row_groups, col_groups, sub_rows * sub_cols, feature_width
    )
    carried = outgoing.shape[0]
    flat_out = outgoing.reshape(
        carried, row_groups * col_groups, sub_rows * sub_cols, feature_width
    )
    arrived = lax.all_to_all(flat_out, ("row", "col"), split_axis=1, concat_axis=1, tiled=True)
    arrived = arrived.reshape(carried, rows * cols, feature_width)
    lattice_queries, lattice_keys, lattice_values = (arrived[0], arrived[1], arrived[2])
    lattice_out = attend(lattice_queries, lattice_keys, lattice_values, None).astype(jnp.bfloat16)
    joint_in = lattice_out.reshape(row_groups * col_groups, sub_rows * sub_cols, feature_width)
    returned = lax.all_to_all(joint_in, ("row", "col"), split_axis=0, concat_axis=0, tiled=True)
    returned = returned.reshape(row_groups, col_groups, sub_rows, sub_cols, feature_width)
    dilated_out = returned.transpose(2, 0, 3, 1, 4).reshape(rows * cols, feature_width)
    weight = blend.reshape(rows * cols, 1)
    mixed = (weight * window_out + (1.0 - weight) * dilated_out.astype(jnp.float32)).astype(
        jnp.bfloat16
    )
    projected = jnp.dot(mixed, w_out, preferred_element_type=jnp.float32)
    branch_out = (
        tokens[0].reshape(rows * cols, feature_width).astype(jnp.float32)
        + modulation[2] * projected
    )
    coefficient = jnp.where(lax.axis_index("branch") == 1, GUIDANCE, 1.0 - GUIDANCE)
    branch_term = (coefficient * branch_out).reshape(rows, cols, feature_width)
    guided = lax.psum_scatter(branch_term, "branch", scatter_dimension=0, tiled=True)
    return guided.astype(jnp.bfloat16)


def solution(mesh):
    in_specs = (
        P("branch", "row", "col", None),
        P(),
        P(),
        P(),
        P("row", "col"),
        P(None, "row", "col"),
    )
    out_specs = P(("row", "branch"), "col", None)
    return jax.shard_map(
        on_device, mesh=mesh, in_specs=in_specs, out_specs=out_specs, check_vma=False
    )
```

profile of v0, /device:TPU:0, one launch (start us, length us, event | category | flops | bytes accessed | tf_op | source)
XLA Modules:
  0.0 293.8 jit_solution(13881071737300400130)
XLA Ops:
  6.5 0.0 copy-start
  6.5 1.7 convert_reduce_fusion
  8.2 1.7 fusion.27
  9.9 0.1 div.25
  10.0 0.0 copy-done.6
  10.1 0.1 rsqrt.12
  10.2 1.8 fusion.31
  11.9 8.4 %convolution_convert_fusion = bf16[512,3456]{1,0:T(8,128)(2,1)S(1)} fusion(bf16[512,1152]{1,0:T(8,128)(2,1)S(1)} %fusion.31, bf16[1152,3456]{1,0:T(8,128)(2,1)} %param.8), kind=kOutput, calls=%fused_computation.16 | convolution fusion | flops 4078632960 | bytes 12681216 | tf_op jit(solution)/shard_map/dot_general | solution.py:42
  20.4 0.3 fusion.54
  20.6 0.0 copy-start.1
  20.7 0.0 copy-start.2
  20.7 1.0 copy-done.1
  21.7 0.4 copy-done.2
  22.1 0.4 copy-done.3
  22.4 0.5 pad_maximum_fusion.1
  22.9 0.3 copy.45
  23.2 2.5 copy.36
  25.7 8.4 %all-to-all-start = ((bf16[3,16,32,1152]{3,2,0,1:T(8,128)(2,1)}), bf16[3,16,32,1152]{3,2,0,1:T(8,128)(2,1)}, u32[]{:S(2)}, u32[]{:S(2)}) async-start(bf16[3,16,32,1152]{3,2,0,1:T(8,128)(2,1)} %copy.36), calls=%async_computation | async-start | bytes 7077888 | tf_op jit(solution)/shard_map/all_to_all | solution.py:119
  34.1 0.0 copy-start.8
  34.1 2.4 pad_maximum_fusion.3
  36.5 1.3 collective-permute-start.1
  37.8 5.4 %collective-permute-start = (bf16[2,4,32,1152]{3,2,1,0:T(8,128)(2,1)}, bf16[2,4,32,1152]{3,2,1,0:T(8,128)(2,1)}, u32[]{:S(2)}, u32[]{:S(2)}) collective-permute-start(bf16[2,4,32,1152]{3,2,1,0:T(8,128)(2,1)} %get-tuple-element.18), channel_id=1, source_target_pairs={{0,8},{1,9},{2,10},{3,11},{4,12},{5,13},{6,14},{7,15},{16,24},{17,... | collective-permute-start | bytes 1769480 | tf_op jit(solution)/shard_map/ppermute | solution.py:23
  43.2 2.4 copy.29
  45.6 0.6 fusion.55
  48.8 28.6 %collective-permute-done.1 = bf16[2,4,32,1152]{3,2,1,0:T(8,128)(2,1)S(1)} collective-permute-done((bf16[2,4,32,1152]{3,2,1,0:T(8,128)(2,1)}, bf16[2,4,32,1152]{3,2,1,0:T(8,128)(2,1)S(1)}, u32[]{:S(2)}, u32[]{:S(2)}) %collective-permute-start.1) | collective-permute-done | bytes 589856 | tf_op jit(solution)/shard_map/ppermute | solution.py:25
  77.4 0.0 collective-permute-done
  77.4 2.6 pad_maximum_fusion.7
  80.0 1.3 collective-permute-start.3
  81.3 5.3 %collective-permute-start.2 = (bf16[2,24,4,1152]{3,2,1,0:T(4,128)(2,1)}, bf16[2,24,4,1152]{3,2,1,0:T(4,128)(2,1)}, u32[]{:S(2)}, u32[]{:S(2)}) collective-permute-start(bf16[2,24,4,1152]{3,2,1,0:T(4,128)(2,1)} %get-tuple-element.10), channel_id=1, source_target_pairs={{0,1},{1,2},{2,3},{3,4},{4,5},{5,6},{6,7},{8,9},{9,10},{10,11},{11... | collective-permute-start | bytes 1327112 | tf_op jit(solution)/shard_map/ppermute | solution.py:23
  86.7 0.1 broadcast_and_fusion
  86.7 0.1 and.74
  86.8 0.0 copy-done.7
  86.8 0.1 mul.76
  86.9 7.7 %collective-permute-done.3 = bf16[2,24,4,1152]{3,2,1,0:T(4,128)(2,1)} collective-permute-done((bf16[2,24,4,1152]{3,2,1,0:T(4,128)(2,1)}, bf16[2,24,4,1152]{3,2,1,0:T(4,128)(2,1)}, u32[]{:S(2)}, u32[]{:S(2)}) %collective-permute-start.3) | collective-permute-done | bytes 442400 | tf_op jit(solution)/shard_map/ppermute | solution.py:25
  94.6 19.0 %collective-permute-done.2 = bf16[2,24,4,1152]{3,2,1,0:T(4,128)(2,1)} collective-permute-done((bf16[2,24,4,1152]{3,2,1,0:T(4,128)(2,1)}, bf16[2,24,4,1152]{3,2,1,0:T(4,128)(2,1)}, u32[]{:S(2)}, u32[]{:S(2)}) %collective-permute-start.2) | collective-permute-done | bytes 442400 | tf_op jit(solution)/shard_map/ppermute | solution.py:23
  113.6 4.5 %pad_maximum_fusion = bf16[2,24,40,1152]{3,2,1,0:T(8,128)(2,1)S(1)} fusion(bf16[2,24,4,1152]{3,2,1,0:T(4,128)(2,1)} %collective-permute-done.3, bf16[2,4,32,1152]{3,2,1,0:T(8,128)(2,1)S(1)} %collective-permute-done.1, bf16[1,16,32,1152]{3,2,1,0:T(8,128)(2,1)} %bitcast.70, bf16[1,16,32,1152]{3,2,1,0:T(8,128)(2,1)} %bitcast.74, ...), kind=kLoop, calls=%fused_computation.18 | loop fusion | flops 26542080 | bytes 8847360 | tf_op jit(solution)/shard_map/concatenate | solution.py:21
  118.1 2.4 fusion.52
  120.6 9.2 %reshape_reshape_squeeze.7 = bf16[960,16,72]{2,1,0:T(8,128)(2,1)} reshape(bf16[1,24,40,1152]{3,2,1,0:T(8,128)(2,1)} %get-tuple-element.9) | data formatting | bytes 4423680 | tf_op jit(solution)/shard_map/reshape;reshape;squeeze | solution.py:55
  129.7 9.1 %reshape_reshape_squeeze.6 = bf16[960,16,72]{2,1,0:T(8,128)(2,1)} reshape(bf16[1,24,40,1152]{3,2,1,0:T(8,128)(2,1)} %get-tuple-element.8) | data formatting | bytes 4423680 | tf_op jit(solution)/shard_map/reshape;reshape;squeeze | solution.py:56
  138.9 19.0 %fusion.57 = (f32[16,512]{1,0:T(8,128)S(1)}, f32[16,512,960]{1,2,0:T(8,128)}) fusion(pred[960]{0:T(1024)(128)(4,1)S(1)} %and.74, bf16[512,16,72]{0,2,1:T(8,128)(2,1)} %bitcast.81, bf16[960,16,72]{2,1,0:T(8,128)(2,1)} %reshape_reshape_squeeze.7), kind=kOutput, calls=%fused_computation.70 | convolution fusion | flops 1163920256 | bytes 34882496 | tf_op jit(solution)/shard_map/sub | solution.py:63
  157.9 0.0 all-to-all-done
  157.9 4.0 %fusion.53 = (bf16[1,16,32,1152]{3,2,0,1:T(8,128)(2,1)}, bf16[1,16,32,1152]{3,2,0,1:T(8,128)(2,1)}, bf16[1,16,32,1152]{3,2,0,1:T(8,128)(2,1)}) fusion(bf16[3,16,32,1152]{3,2,0,1:T(8,128)(2,1)} %all-to-all-done), kind=kLoop, calls=%fused_computation.66 | loop fusion | bytes 7077888 | tf_op jit(solution)/shard_map/slice | solution.py:121
  161.9 5.7 %reshape_squeeze.12 = bf16[512,16,72]{2,1,0:T(8,128)(2,1)} reshape(bf16[1,16,32,1152]{3,2,0,1:T(8,128)(2,1)} %get-tuple-element.13) | data formatting | bytes 2359296 | tf_op jit(solution)/shard_map/reshape;squeeze | solution.py:55
  167.6 5.7 %reshape_squeeze.11 = bf16[512,16,72]{2,1,0:T(8,128)(2,1)} reshape(bf16[1,16,32,1152]{3,2,0,1:T(8,128)(2,1)} %get-tuple-element.14) | data formatting | bytes 2359296 | tf_op jit(solution)/shard_map/reshape;squeeze | solution.py:54
  173.3 10.5 %fusion.33 = f32[16,512,512]{1,2,0:T(8,128)} fusion(bf16[512,16,72]{2,1,0:T(8,128)(2,1)} %reshape_squeeze.12, bf16[512,16,72]{2,1,0:T(8,128)(2,1)} %reshape_squeeze.11), kind=kOutput, calls=%fused_computation.39 | convolution fusion | flops 603979776 | bytes 19136512 | tf_op jit(solution)/shard_map/qhd,khd->hqk/dot_general | solution.py:57
  183.8 12.6 %fusion.56 = f32[16,512]{1,0:T(8,128)S(1)} fusion(f32[16,512,512]{1,2,0:T(8,128)} %fusion.33), kind=kOutput, calls=%fused_computation.69 | output fusion | flops 16777728 | bytes 16809984 | tf_op jit(solution)/shard_map/sub | solution.py:63
  196.4 5.7 %reshape_squeeze.10 = bf16[512,16,72]{2,1,0:T(8,128)(2,1)} reshape(bf16[1,16,32,1152]{3,2,0,1:T(8,128)(2,1)} %get-tuple-element.12) | data formatting | bytes 2359296 | tf_op jit(solution)/shard_map/reshape;squeeze | solution.py:56
  202.1 15.1 %fusion.39 = bf16[512,16,72]{0,2,1:T(8,128)(2,1)} fusion(f32[16,512]{1,0:T(8,128)S(1)} %fusion.56, bf16[512,16,72]{2,1,0:T(8,128)(2,1)} %reshape_squeeze.10, f32[16,512,512]{1,2,0:T(8,128)} %fusion.33), kind=kOutput, calls=%fused_computation.44 | convolution fusion | flops 625549824 | bytes 19169280 | tf_op jit(solution)/shard_map/hqk,khd->qhd/dot_general | solution.py:65
  217.3 4.3 %copy.41 = bf16[512,16,72]{2,1,0:T(8,128)(2,1)} copy(bf16[512,16,72]{0,2,1:T(8,128)(2,1)} %fusion.39) | data formatting | bytes 2359296 | tf_op jit(solution)/shard_map/convert_element_type | solution.py:122
  221.6 4.6 %convert_element_type.64 = bf16[16,32,1152]{2,1,0:T(8,128)(2,1)} reshape(bf16[512,16,72]{2,1,0:T(8,128)(2,1)} %copy.41) | data formatting | bytes 2359296 | tf_op jit(solution)/shard_map/convert_element_type | solution.py:122
  226.2 13.8 %all-to-all-start.1 = ((bf16[16,32,1152]{2,1,0:T(8,128)(2,1)}), bf16[16,32,1152]{2,1,0:T(8,128)(2,1)}, u32[]{:S(2)}, u32[]{:S(2)}) async-start(bf16[16,32,1152]{2,1,0:T(8,128)(2,1)} %convert_element_type.64), calls=%async_computation.1 | async-start | bytes 2359296 | tf_op jit(solution)/shard_map/all_to_all | solution.py:124
  240.0 0.0 reduce-scatter.2.cloned.1.call-start
  240.0 15.7 %fusion.6 = f32[16,72,512]{2,1,0:T(8,128)} fusion(f32[16,512,960]{1,2,0:T(8,128)} %get-tuple-element.25, f32[16,512]{1,0:T(8,128)S(1)} %get-tuple-element.24, bf16[960,16,72]{2,1,0:T(8,128)(2,1)} %reshape_reshape_squeeze.6), kind=kOutput, calls=%fused_computation.11 | convolution fusion | flops 1148190720 | bytes 36061184 | tf_op jit(solution)/shard_map/hqk,khd->qhd/dot_general | solution.py:65
  255.7 3.1 %copy.32 = f32[512,1152]{1,0:T(8,128)} copy(f32[512,1152]{0,1:T(8,128)} %bitcast.80) | data formatting | bytes 4718592 | tf_op jit(solution)/shard_map/reshape | solution.py:66
  258.8 10.0 %all-to-all-done.1 = bf16[16,32,1152]{2,1,0:T(8,128)(2,1)} async-done(((bf16[16,32,1152]{2,1,0:T(8,128)(2,1)}), bf16[16,32,1152]{2,1,0:T(8,128)(2,1)}, u32[]{:S(2)}, u32[]{:S(2)}) %all-to-all-start.1) | async-done | bytes 1179680 | tf_op jit(solution)/shard_map/all_to_all | solution.py:124
  268.8 1.7 copy.42
  270.5 0.2 copy.43
  270.7 1.4 copy-done.5
  272.1 0.4 fusion.25
  272.5 0.9 copy-done.4
  273.4 3.3 %fusion.23 = f32[512,1152]{1,0:T(8,128)} fusion(bf16[512,1152]{1,0:T(8,128)(2,1)S(1)} %fusion.25, bf16[1152,1152]{1,0:T(8,128)(2,1)S(1)} %copy-done, f32[1152]{0:T(1024)S(1)} %get-tuple-element.5, f32[]{:T(128)S(6)} %select_n.8, bf16[512,1152]{1,0:T(8,128)(2,1)S(1)} %bitcast.77), kind=kOutput, calls=%fused_computation.26 | convolution fusion | flops 1361313792 | bytes 7377412 | tf_op jit(solution)/shard_map/dot_general | solution.py:131
  276.7 0.0 reduce-scatter.2.cloned.1.call-update
  276.7 8.1 %reduce-scatter.2.cloned.1.call-done = f32[8,32,1152]{2,1,0:T(8,128)} async-done(((f32[16,32,1152]{2,1,0:T(8,128)}), f32[8,32,1152]{2,1,0:T(8,128)}) %reduce-scatter.2.cloned.1.call-update) | async-done | bytes 1179664 | tf_op jit(solution)/shard_map/reduce_scatter | solution.py:138
  284.8 2.1 convert_element_type.70
  (13 shorter events, 0.1 us)
Async XLA Ops:
  6.5 265.9 %copy-start = (bf16[1152,1152]{1,0:T(8,128)(2,1)S(1)}, bf16[1152,1152]{1,0:T(8,128)(2,1)}, u32[]{:S(2)}) copy-start(bf16[1152,1152]{1,0:T(8,128)(2,1)} %param.9) | copy-start | bytes 7962628
  6.5 3.5 %copy-start.6 = (f32[3,1152]{1,0:T(4,128)S(1)}, f32[3,1152]{1,0:T(4,128)}, u32[]{:S(2)}) copy-start(f32[3,1152]{1,0:T(4,128)} %param.7) | copy-start | bytes 41476
  20.6 1.0 copy-start.1
  20.7 1.4 copy-start.2
  20.7 1.8 copy-start.3
  25.7 132.2 %all-to-all-start = ((bf16[3,16,32,1152]{3,2,0,1:T(8,128)(2,1)}), bf16[3,16,32,1152]{3,2,0,1:T(8,128)(2,1)}, u32[]{:S(2)}, u32[]{:S(2)}) async-start(bf16[3,16,32,1152]{3,2,0,1:T(8,128)(2,1)} %copy.36), calls=%async_computation | async-start | bytes 7077888 | tf_op jit(solution)/shard_map/all_to_all | solution.py:119
  34.1 11.5 %copy-start.8 = (s32[4,1,1]{0,2,1:T(1,128)S(1)}, s32[4,1,1]{0,2,1:T(1,128)}, u32[]{:S(2)}) copy-start(s32[4,1,1]{0,2,1:T(1,128)} %param.11) | copy-start | bytes 52
  36.5 40.9 %collective-permute-start.1 = (bf16[2,4,32,1152]{3,2,1,0:T(8,128)(2,1)}, bf16[2,4,32,1152]{3,2,1,0:T(8,128)(2,1)S(1)}, u32[]{:S(2)}, u32[]{:S(2)}) collective-permute-start(bf16[2,4,32,1152]{3,2,1,0:T(8,128)(2,1)} %get-tuple-element.19), channel_id=1, source_target_pairs={{8,0},{9,1},{10,2},{11,3},{12,4},{13,5},{14,6},{15,7},{24,16},{25,... | collective-permute-start | bytes 1769480 | tf_op jit(solution)/shard_map/ppermute | solution.py:25
  37.8 39.6 %collective-permute-start = (bf16[2,4,32,1152]{3,2,1,0:T(8,128)(2,1)}, bf16[2,4,32,1152]{3,2,1,0:T(8,128)(2,1)}, u32[]{:S(2)}, u32[]{:S(2)}) collective-permute-start(bf16[2,4,32,1152]{3,2,1,0:T(8,128)(2,1)} %get-tuple-element.18), channel_id=1, source_target_pairs={{0,8},{1,9},{2,10},{3,11},{4,12},{5,13},{6,14},{7,15},{16,24},{17,... | collective-permute-start | bytes 1769480 | tf_op jit(solution)/shard_map/ppermute | solution.py:23
  45.6 41.2 %copy-start.7 = (f32[16,32]{1,0:T(8,128)S(1)}, f32[16,32]{1,0:T(8,128)}, u32[]{:S(2)}) copy-start(f32[16,32]{1,0:T(8,128)} %param.10) | copy-start | bytes 6148
  80.0 14.6 %collective-permute-start.3 = (bf16[2,24,4,1152]{3,2,1,0:T(4,128)(2,1)}, bf16[2,24,4,1152]{3,2,1,0:T(4,128)(2,1)}, u32[]{:S(2)}, u32[]{:S(2)}) collective-permute-start(bf16[2,24,4,1152]{3,2,1,0:T(4,128)(2,1)} %get-tuple-element.11), channel_id=1, source_target_pairs={{1,0},{2,1},{3,2},{4,3},{5,4},{6,5},{7,6},{9,8},{10,9},{11,10},{12... | collective-permute-start | bytes 1327112 | tf_op jit(solution)/shard_map/ppermute | solution.py:25
  81.3 32.3 %collective-permute-start.2 = (bf16[2,24,4,1152]{3,2,1,0:T(4,128)(2,1)}, bf16[2,24,4,1152]{3,2,1,0:T(4,128)(2,1)}, u32[]{:S(2)}, u32[]{:S(2)}) collective-permute-start(bf16[2,24,4,1152]{3,2,1,0:T(4,128)(2,1)} %get-tuple-element.10), channel_id=1, source_target_pairs={{0,1},{1,2},{2,3},{3,4},{4,5},{5,6},{6,7},{8,9},{9,10},{10,11},{11... | collective-permute-start | bytes 1327112 | tf_op jit(solution)/shard_map/ppermute | solution.py:23
  226.2 42.6 %all-to-all-start.1 = ((bf16[16,32,1152]{2,1,0:T(8,128)(2,1)}), bf16[16,32,1152]{2,1,0:T(8,128)(2,1)}, u32[]{:S(2)}, u32[]{:S(2)}) async-start(bf16[16,32,1152]{2,1,0:T(8,128)(2,1)} %convert_element_type.64), calls=%async_computation.1 | async-start | bytes 2359296 | tf_op jit(solution)/shard_map/all_to_all | solution.py:124
  240.0 44.8 %reduce-scatter.2.cloned.1.call-start = ((), (), s32[]{:S(2)}) async-start(), calls=%async_computation.3 | async-start | bytes 3538944 | tf_op jit(solution)/shard_map/reduce_scatter | solution.py:138
  270.5 1.7 copy-start.5
  272.1 1.3 copy-start.4
Sparse Core Ops, SparseCore 0:
  276.8 7.9 reduce-scatter.1
where the time goes:
time: 295 us; the launch traced here: 294 us
  waiting for transfers between devices  73.4 us (25%)
  matrix products  72.1 us (24%)
  local copies, waits for them, and re-layouts  66.3 us (22%)
  starting transfers between devices  35.5 us (12%)
  other arithmetic  30.4 us (10%)
  between operations  16.1 us (5%)
    ppermute x2, waiting for transfers between devices, with_halo(): lax.ppermute(head, axis, [((i + 1) % count, i) for i in range(ends)])  36.3 us
    dot_general x2, matrix products, attend(): jnp.einsum('hqk,khd->qhd', weights, value_heads, preferred_element_type=j...  30.8 us
    sub x1, matrix products, attend(): powers = jnp.exp(scores - row_max)  19 us
    ppermute x2, waiting for transfers between devices, with_halo(): lax.ppermute(tail, axis, [(i, (i + 1) % count) for i in range(ends)])  19 us
    another operation x2, local copies, waits for them, and re-layouts, attend(): key_heads = keys.reshape(key_count, HEADS, head_size)  14.9 us
    another operation x2, local copies, waits for them, and re-layouts, attend(): value_heads = values.reshape(key_count, HEADS, head_size)  14.9 us
    all_to_all x1, starting transfers between devices, on_device(): lax.all_to_all(joint_in, ('row', 'col'), split_axis=0, concat_axis=0, til...  13.8 us
    sub x1, other arithmetic, attend(): powers = jnp.exp(scores - row_max)  12.6 us
  transfers between devices with their start and end apart: 7, of which 5 were waited for; matrix products, arithmetic and copies ran while one was open for 24% of the time, Pallas kernels for 0%

commit v1 on v0

--- a/solution.py
+++ b/solution.py
@@ -1,8 +1,12 @@
+import functools
 import math
 
 import jax
 import jax.numpy as jnp
+import numpy as np
 from jax import lax
+from jax.experimental import pallas as pl
+from jax.experimental.pallas import tpu as pltpu
 from jax.sharding import PartitionSpec as P
 
 HEADS = 16
@@ -139,6 +143,416 @@
     return guided.astype(jnp.bfloat16)
 
 
+MESH = pl.DeviceIdType.MESH
+LANES = 128
+CHUNK = 128
+
+
+def halo_slots(rows, cols):
+    side, edge, corner = HALO * cols, rows * HALO, HALO * HALO
+    sizes = [(side, 1, 0), (edge, 0, -1), (edge, 0, 1), (corner, 1, -1), (corner, 1, 1)]
+    slots, start = [], 0
+    for count, flip, step in sizes:
+        slots.append((start, count, flip, step))
+        start += count
+    return slots, start
+
+
+def selections(rows, cols, row_groups, col_groups, padded):
+    tile = rows * cols
+    sub_rows, sub_cols = rows // row_groups, cols // col_groups
+    natural = np.arange(tile).reshape(sub_rows, row_groups, sub_cols, col_groups)
+    phased = natural.transpose(1, 3, 0, 2).reshape(-1)
+    grid = np.arange(tile).reshape(rows, cols)
+    slots, total = halo_slots(rows, cols)
+    chosen = [phased]
+    offsets = []
+    for row in range(2):
+        sent, where = [], []
+        for _, count, flip, step in slots:
+            picked = grid
+            if flip:
+                picked = picked[rows - HALO :] if row == 0 else picked[:HALO]
+            if step:
+                picked = picked[:, :HALO] if step < 0 else picked[:, cols - HALO :]
+            sent.append(picked.reshape(-1))
+            r = np.arange(rows)
+            if flip:
+                r = np.arange(rows, rows + HALO) if row == 0 else np.arange(-HALO, 0)
+            c = np.arange(cols)
+            if step:
+                c = np.arange(cols, cols + HALO) if step < 0 else np.arange(-HALO, 0)
+            rr, cc = np.meshgrid(r, c, indexing="ij")
+            where.append(np.stack([rr.reshape(-1), cc.reshape(-1)], axis=1))
+        chosen.append(np.concatenate(sent))
+        spread = np.full((padded, 2), -1000, np.int32)
+        spread[:total] = np.concatenate(where)
+        offsets.append(spread)
+    chosen = np.concatenate(chosen)
+    select = (chosen[:, None] == np.arange(tile)[None, :]).astype(np.float32)
+    half = tile // 2
+    per = tile // (row_groups * col_groups)
+    front = phased.reshape(row_groups * col_groups, per)[:, : per // 2].reshape(-1)
+    restore = (front[None, :] == np.arange(half)[:, None]).astype(np.float32)
+    return select, restore, np.concatenate(offsets)
+
+
+def fused(
+    dims,
+    x_ref, mod_ref, w_ref, wout_ref, blend_ref, reach_ref, select_ref, restore_ref, offs_ref,
+    out_ref,
+    normed, phased, halo_out, halo_in, lattice, near, far,
+    dil, dil_other, combined, returned, win, win_other, rest,
+    a2a_send, a2a_recv, halo_send, halo_recv, ret_send, ret_recv, pair_send, pair_recv,
+):
+    rows, cols, row_groups, col_groups = dims
+    tile = rows * cols
+    half = tile // 2
+    groups = row_groups * col_groups
+    width = x_ref.shape[-1]
+    size = width // HEADS
+    slots, sent = halo_slots(rows, cols)
+    padded = halo_in.shape[0]
+    branch = lax.axis_index("branch")
+    row = lax.axis_index("row")
+    col = lax.axis_index("col")
+    me = row * col_groups + col
+    other = 1 - branch
+
+    def place(p):
+        return (branch, p // col_groups, p % col_groups)
+
+    barrier = pltpu.get_barrier_semaphore()
+
+    def greet(k, carry):
+        pl.semaphore_signal(
+            barrier, inc=1, device_id=place((me + k) % groups), device_id_type=MESH
+        )
+        return carry
+
+    lax.fori_loop(1, groups, greet, 0)
+    pl.semaphore_signal(barrier, inc=1, device_id=(other, row, col), device_id_type=MESH)
+
+    gain = 1.0 + mod_ref[1:2, :]
+    shift = mod_ref[0:1, :]
+
+    def norm(i, carry):
+        at = pl.ds(pl.multiple_of(i * CHUNK, CHUNK), CHUNK)
+        widened = x_ref[at, :].astype(jnp.float32)
+        centered = widened - jnp.mean(widened, axis=-1, keepdims=True)
+        variance = jnp.mean(centered * centered, axis=-1, keepdims=True)
+        scaled = centered * lax.rsqrt(variance + 1e-06)
+        normed[at, :] = (scaled * gain + shift).astype(jnp.bfloat16)
+        return carry
+
+    lax.fori_loop(0, tile // CHUNK, norm, 0)
+
+    start = pl.multiple_of(tile + row * sent, 16)
+    halo_out[...] = jnp.dot(
+        select_ref[pl.ds(start, sent), :], normed[...], preferred_element_type=jnp.float32
+    ).astype(jnp.bfloat16)
+
+    pl.semaphore_wait(barrier, groups)
+
+    def pair_copy(k, source, target):
+        return pltpu.make_async_remote_copy(
+            src_ref=source, dst_ref=target, send_sem=pair_send.at[k], recv_sem=pair_recv.at[k],
+            device_id=(other, row, col), device_id_type=MESH,
+        )
+
+    halo_copies = []
+    for k, (begin, count, flip, step) in enumerate(slots):
+        to = (
+            branch,
+            (row + flip) % row_groups,
+            (col + step + col_groups) % col_groups,
+        )
+        copy = pltpu.make_async_remote_copy(
+            src_ref=halo_out.at[pl.ds(begin, count)], dst_ref=halo_in.at[pl.ds(begin, count)],
+            send_sem=halo_send.at[k], recv_sem=halo_recv.at[k],
+            device_id=to, device_id_type=MESH,
+        )
+        copy.start()
+        halo_copies.append(copy)
+
+    per = tile // groups
+    blocks = CHUNK // per
+
+    def arrange(i, carry):
+        at = pl.ds(pl.multiple_of(i * CHUNK, CHUNK), CHUNK)
+        picked = jnp.dot(select_ref[at, :], normed[...], preferred_element_type=jnp.float32)
+        phased[pl.ds(i * blocks, blocks)] = picked.astype(jnp.bfloat16).reshape(blocks, per, width)
+        return carry
+
+    lax.fori_loop(0, tile // CHUNK, arrange, 0)
+
+    def outward(k):
+        to = (me + k) % groups
+        return pltpu.make_async_remote_copy(
+            src_ref=phased.at[to], dst_ref=lattice.at[me],
+            send_sem=a2a_send.at[k], recv_sem=a2a_recv.at[k],
+            device_id=place(to), device_id_type=MESH,
+        )
+
+    def inward(k):
+        return pltpu.make_async_remote_copy(
+            src_ref=phased.at[me], dst_ref=lattice.at[(me + groups - k) % groups],
+            send_sem=a2a_send.at[k], recv_sem=a2a_recv.at[k],
+            device_id=place((me + k) % groups), device_id_type=MESH,
+        )
+
+    def send_out(k, carry):
+        outward(k).start()
+        return carry
+
+    lax.fori_loop(1, groups, send_out, 0)
+    tokens_copy = pair_copy(0, x_ref.at[pl.ds(pl.multiple_of(other * half, half), half)], rest)
+    tokens_copy.start()
+    lattice[me] = phased[me]
+
+    log_scale = math.log2(math.e) / math.sqrt(size)
+    lane = lax.broadcasted_iota(jnp.int32, (1, LANES), 1)
+
+    def clear(ref, begin, count, weight):
+        mark = jnp.where(lane == size, weight, 0.0).astype(jnp.bfloat16)
+        mark = jnp.broadcast_to(mark, (count, LANES))
+        blank = jnp.zeros((count, LANES), jnp.bfloat16)
+
+        def body(h, carry):
+            at = pl.ds(begin, count)
+            if begin == 0:
+                ref[h, at, :] = blank
+            ref[HEADS + h, at, :] = blank
+            ref[2 * HEADS + h, at, :] = mark
+            return carry
+
+        lax.fori_loop(0, HEADS, body, 0)
+
+    def spread(ref, part, at, value):
+        value = value.astype(jnp.bfloat16)
+        for h in range(HEADS):
+            ref[part * HEADS + h, at, 0:size] = value[:, h * size : (h + 1) * size]
+
+    def weights_of(part):
+        return w_ref[:, pl.ds(pl.multiple_of(part * width, LANES), width)]
+
+    piece = 2 * CHUNK
+
+    def project_all(ref, load):
+        clear(ref, 0, tile, jnp.ones((1, 1), jnp.float32))
+
+        def body(step, carry):
+            part = step // (tile // piece)
+            i = step % (tile // piece)
+            at = pl.ds(pl.multiple_of(i * piece, piece), piece)
+            y = jnp.dot(load(i, at), weights_of(part), preferred_element_type=jnp.float32)
+            factor = jnp.where(part == 0, log_scale, 1.0)
+            spread(ref, part, at, y * factor)
+            return carry
+
+        lax.fori_loop(0, 3 * (tile // piece), body, 0)
+
+    wide = piece // per
+    project_all(near, lambda i, at: phased[pl.ds(i * wide, wide)].reshape(piece, width))
+
+    offset_at = pl.ds(pl.multiple_of(row * padded, padded), padded)
+    r_off = offs_ref[offset_at, 0:1]
+    c_off = offs_ref[offset_at, 1:2]
+    left = jnp.where(col == 0, 0, reach_ref[2])
+    right = jnp.where(col == col_groups - 1, 0, reach_ref[3])
+    allowed = (
+        (r_off >= -reach_ref[0])
+        & (r_off < rows + reach_ref[1])
+        & (c_off >= -left)
+        & (c_off < cols + right)
+    )
+    allow = jnp.where(allowed, 1.0, 0.0)
+    halo_in[sent:padded, :] = jnp.zeros((padded - sent, width), jnp.bfloat16)
+    clear(near, tile, padded, allow)
+    for copy in halo_copies:
+        copy.wait_recv()
+    halo_at = pl.ds(tile, padded)
+
+    def project_halo(part, carry):
+        weight = weights_of(part)
+        y = jnp.dot(halo_in[...], weight, preferred_element_type=jnp.float32)
+        spare = jnp.dot(normed[0:16, :], weight, preferred_element_type=jnp.float32)[0:1, :]
+        spare = spare * jnp.where(part == 1, 1.0, 0.0)
+        spread(near, part, halo_at, jnp.where(allow > 0.5, y, spare))
+        return carry
+
+    lax.fori_loop(1, 3, project_halo, 0)
+
+    def attend_heads(ref, first, last):
+        def body(h, carry):
+            keys = ref[HEADS + h]
+            values = ref[2 * HEADS + h]
+            for r in range(tile // CHUNK):
+                at = pl.ds(r * CHUNK, CHUNK)
+                scores = lax.dot_general(
+                    ref[h, at, :], keys, (((1,), (1,)), ((), ())),
+                    preferred_element_type=jnp.float32,
+                )
+                powers = jnp.exp2(scores - jnp.max(scores, axis=-1, keepdims=True))
+                got = jnp.dot(
+                    powers.astype(jnp.bfloat16), values, preferred_element_type=jnp.float32
+                )
+                ref[h, at, :] = (got * (1.0 / got[:, size : size + 1])).astype(jnp.bfloat16)
+            return carry
+
+        lax.fori_loop(first, last, body, 0)
+
+    def gather_heads(ref, target):
+        count = target.shape[0] * CHUNK // tile
+
+        def body(i, carry):
+            at = pl.ds(pl.multiple_of(i * CHUNK, CHUNK), CHUNK)
+            to = pl.ds(i * count, count)
+            for h in range(HEADS):
+                value = ref[h, at, 0:size].reshape(count, 2, per // 2, size)
+                target[to, :, :, h * size : (h + 1) * size] = value
+            return carry
+
+        lax.fori_loop(0, tile // CHUNK, body, 0)
+
+    attend_heads(near, 0, HEADS // 2)
+
+    def take_in(k, carry):
+        inward(k).wait_recv()
+        return carry
+
+    lax.fori_loop(1, groups, take_in, 0)
+    project_all(far, lambda i, at: lattice[pl.ds(i * wide, wide)].reshape(piece, width))
+    attend_heads(far, 0, HEADS)
+    gather_heads(far, dil)
+    dil_copy = pair_copy(1, dil.at[:, other], dil_other)
+    dil_copy.start()
+    dil_copy.wait_recv()
+    mine = jnp.where(branch == 1, GUIDANCE, 1.0 - GUIDANCE)
+    theirs = 1.0 - mine
+
+    def combine(i, carry):
+        combined[i] = (
+            mine * dil[i, branch].astype(jnp.float32) + theirs * dil_other[i].astype(jnp.float32)
+        ).astype(jnp.bfloat16)
+        return carry
+
+    lax.fori_loop(0, groups, combine, 0)
+
+    def back(k):
+        to = (me + k) % groups
+        return pltpu.make_async_remote_copy(
+            src_ref=combined.at[to], dst_ref=returned.at[me],
+            send_sem=ret_send.at[k], recv_sem=ret_recv.at[k],
+            device_id=place(to), device_id_type=MESH,
+        )
+
+    def back_in(k):
+        return pltpu.make_async_remote_copy(
+            src_ref=combined.at[me], dst_ref=returned.at[(me + groups - k) % groups],
+            send_sem=ret_send.at[k], recv_sem=ret_recv.at[k],
+            device_id=place((me + k) % groups), device_id_type=MESH,
+        )
+
+    def send_back(k, carry):
+        back(k).start()
+        return carry
+
+    lax.fori_loop(1, groups, send_back, 0)
+    returned[me] = combined[me]
+
+    attend_heads(near, HEADS // 2, HEADS)
+    gather_heads(near, win)
+    win_copy = pair_copy(2, win.at[:, other], win_other)
+    win_copy.start()
+
+    def take_back(k, carry):
+        back_in(k).wait_recv()
+        return carry
+
+    lax.fori_loop(1, groups, take_back, 0)
+    win_copy.wait_recv()
+    tokens_copy.wait_recv()
+
+    weight = blend_ref[pl.ds(pl.multiple_of(branch * half, half), half), :]
+    window = mine * win[:, branch].astype(jnp.float32) + theirs * win_other[...].astype(jnp.float32)
+    window = window.reshape(half, width)
+    dilated = returned[...].astype(jnp.float32).reshape(half, width)
+    mixed = (weight * window + (1.0 - weight) * dilated).astype(jnp.bfloat16)
+    mixed = jnp.dot(restore_ref[...], mixed, preferred_element_type=jnp.float32)
+    projected = jnp.dot(
+        mixed.astype(jnp.bfloat16), wout_ref[...], preferred_element_type=jnp.float32
+    )
+    own = x_ref[pl.ds(pl.multiple_of(branch * half, half), half), :].astype(jnp.float32)
+    base = mine * own + theirs * rest[...].astype(jnp.float32)
+    out_ref[...] = (base + mod_ref[2:3, :] * projected).astype(jnp.bfloat16)
+
+    for copy in halo_copies:
+        copy.wait_send()
+    for copy in (tokens_copy, dil_copy, win_copy):
+        copy.wait_send()
+
+    def finish(k, carry):
+        outward(k).wait_send()
+        back(k).wait_send()
+        return carry
+
+    lax.fori_loop(1, groups, finish, 0)
+
+
+def on_device_fused(dims, tokens, modulation, wqkv, w_out, blend, reach):
+    rows, cols, row_groups, col_groups = dims
+    tile = rows * cols
+    half = tile // 2
+    groups = row_groups * col_groups
+    per = tile // groups
+    width = tokens.shape[-1]
+    _, sent = halo_slots(rows, cols)
+    padded = -(-(tile + sent) // LANES) * LANES - tile
+    select, restore, offsets = selections(rows, cols, row_groups, col_groups, padded)
+    order = blend.reshape(2, rows // row_groups // 2, row_groups, cols // col_groups, col_groups)
+    order = order.transpose(0, 2, 4, 1, 3).reshape(tile, 1)
+    bf16 = jnp.bfloat16
+    vmem = pl.BlockSpec(memory_space=pltpu.VMEM)
+    out = pl.pallas_call(
+        functools.partial(fused, dims),
+        out_shape=jax.ShapeDtypeStruct((half, width), bf16),
+        in_specs=[vmem] * 5 + [pl.BlockSpec(memory_space=pltpu.SMEM)] + [vmem] * 3,
+        out_specs=vmem,
+        scratch_shapes=[
+            pltpu.VMEM((tile, width), bf16),
+            pltpu.VMEM((groups, per, width), bf16),
+            pltpu.VMEM((sent, width), bf16),
+            pltpu.VMEM((padded, width), bf16),
+            pltpu.VMEM((groups, per, width), bf16),
+            pltpu.VMEM((3 * HEADS, tile + padded, LANES), bf16),
+            pltpu.VMEM((3 * HEADS, tile, LANES), bf16),
+            pltpu.VMEM((groups, 2, per // 2, width), bf16),
+            pltpu.VMEM((groups, per // 2, width), bf16),
+            pltpu.VMEM((groups, per // 2, width), bf16),
+            pltpu.VMEM((groups, per // 2, width), bf16),
+            pltpu.VMEM((groups, 2, per // 2, width), bf16),
+            pltpu.VMEM((groups, per // 2, width), bf16),
+            pltpu.VMEM((half, width), bf16),
+            pltpu.SemaphoreType.DMA((groups,)),
+            pltpu.SemaphoreType.DMA((groups,)),
+            pltpu.SemaphoreType.DMA((5,)),
+            pltpu.SemaphoreType.DMA((5,)),
+            pltpu.SemaphoreType.DMA((groups,)),
+            pltpu.SemaphoreType.DMA((groups,)),
+            pltpu.SemaphoreType.DMA((3,)),
+            pltpu.SemaphoreType.DMA((3,)),
+        ],
+        compiler_params=pltpu.CompilerParams(
+            collective_id=0, has_side_effects=True, vmem_limit_bytes=60 * 1024 * 1024
+        ),
+    )(
+        tokens.reshape(tile, width), modulation, wqkv, w_out, order, reach.reshape(4),
+        jnp.asarray(select, bf16), jnp.asarray(restore, bf16), jnp.asarray(offsets),
+    )
+    return out.reshape(rows // 2, cols, width)
+
+
 def solution(mesh):
     in_specs = (
         P("branch", "row", "col", None),
@@ -149,6 +563,22 @@
         P(None, "row", "col"),
     )
     out_specs = P(("row", "branch"), "col", None)
-    return jax.shard_map(
-        on_device, mesh=mesh, in_specs=in_specs, out_specs=out_specs, check_vma=False
-    )
+    row_groups, col_groups = mesh.shape["row"], mesh.shape["col"]
+
+    def whole(tokens, *others):
+        rows, cols = tokens.shape[1] // row_groups, tokens.shape[2] // col_groups
+        groups = row_groups * col_groups
+        fits = (
+            row_groups == 2
+            and col_groups > 2
+            and (rows * cols) % (32 * groups) == 0
+            and rows // row_groups % 2 == 0
+        )
+        body = on_device
+        if fits:
+            body = functools.partial(on_device_fused, (rows, cols, row_groups, col_groups))
+        return jax.shard_map(
+            body, mesh=mesh, in_specs=in_specs, out_specs=out_specs, check_vma=False
+        )(tokens, *others)
+
+    return whole

time: 295 us -> 104 us (0.35)
  Pallas kernels: 0 us -> 99.7 us
  waiting for transfers between devices: 73.4 us -> 0 us
  matrix products: 72.1 us -> 0 us
  local copies, waits for them, and re-layouts: 66.3 us -> 3.72 us
  starting transfers between devices: 35.5 us -> 0 us
  other arithmetic: 30.4 us -> 0 us
  between operations: 16.1 us -> 0.01 us
    pallas_call x0 -> x1, Pallas kernels: none -> 99.7 us  [on_device_fused(): pl.pallas_call(functools.partial(fused, dims), out_shape=jax.ShapeDtypeSt...]
    ppermute x4 -> x0, waiting for transfers between devices: 55.3 us -> none  [the longest x2 36.3 us: with_halo(): lax.ppermute(head, axis, [((i + 1) % count, i) for i in range(ends)])]
    dot_general x5 -> x0, matrix products: 53 us -> none  [the longest x2 30.8 us: attend(): jnp.einsum('hqk,khd->qhd', weights, value_heads, preferred_element_type=j...]
    another operation x7 -> x0, local copies, waits for them, and re-layouts: 38.3 us -> none  [the longest x2 14.9 us: attend(): key_heads = keys.reshape(key_count, HEADS, head_size)]
    all_to_all x2 -> x0, starting transfers between devices: 22.1 us -> none  [the longest x1 13.8 us: on_device(): lax.all_to_all(joint_in, ('row', 'col'), split_axis=0, concat_axis=0, til...]
    sub x1 -> x0, matrix products: 19 us -> none  [attend(): powers = jnp.exp(scores - row_max)]
    ppermute x4 -> x0, starting transfers between devices: 13.3 us -> none  [the longest x2 10.8 us: with_halo(): lax.ppermute(tail, axis, [(i, (i + 1) % count) for i in range(ends)])]
    sub x2 -> x0, other arithmetic: 12.6 us -> none  [the longest x1 12.6 us: attend(): powers = jnp.exp(scores - row_max)]
  transfers between devices with their start and end apart: 7 -> 0, of which waited for: 5 -> 0; matrix products, arithmetic and copies ran while one was open for 24% -> 0% of each run, Pallas kernels for 0% -> 0%
where the time goes in v1:
time: 104 us; the launch traced here: 103 us
  Pallas kernels  99.7 us (96%)
  local copies, waits for them, and re-layouts  3.72 us (4%)
    pallas_call x1, Pallas kernels, on_device_fused(): pl.pallas_call(functools.partial(fused, dims), out_shape=jax.ShapeDtypeSt...  99.7 us

profile of v1, /device:TPU:0, one launch (start us, length us, event | category | flops | bytes accessed | tf_op | source)
XLA Modules:
  0.0 103.4 jit_solution(6166584346658953257)
XLA Ops:
  0.0 0.8 reshape.16
  0.8 0.2 copy.11
  1.0 0.8 reshape.20.blend_ref
  1.8 99.7 %shard_map.91 = bf16[256,1152]{1,0:T(8,128)(2,1)} custom-call(bf16[512,1152]{1,0:T(8,128)(2,1)} %bitcast.5, f32[3,1152]{1,0:T(4,128)} %mod_ref.1, bf16[1152,3456]{1,0:T(8,128)(2,1)} %w_ref.1, bf16[1152,1152]{1,0:T(8,128)(2,1)} %wout_ref.1, f32[512,1]{1,0:T(8,128)} %reshape.20.blend_ref, s32[4]{0:T(128)} %bitcast.7, ...), custom_call_target="tpu_custom_call" | custom-call | tf_op jit(solution)/shard_map/pallas_call | solution.py:517
  101.5 1.9 %copy.14 = bf16[8,32,1152]{2,1,0:T(8,128)(2,1)} copy(bf16[8,32,1152]{2,1,0:T(8,128)(2,1)} %bitcast.4) | data formatting | bytes 1179648

commit v2 on v1

--- a/solution.py
+++ b/solution.py
@@ -194,15 +194,17 @@
     per = tile // (row_groups * col_groups)
     front = phased.reshape(row_groups * col_groups, per)[:, : per // 2].reshape(-1)
     restore = (front[None, :] == np.arange(half)[:, None]).astype(np.float32)
+    offsets.append(np.stack([front // cols, front % cols], axis=1).astype(np.int32))
     return select, restore, np.concatenate(offsets)
 
 
 def fused(
     dims,
-    x_ref, mod_ref, w_ref, wout_ref, blend_ref, reach_ref, select_ref, restore_ref, offs_ref,
+    x_ref, mod_ref, w_hbm, wout_hbm, blend_ref, reach_ref, select_ref, restore_ref, offs_ref,
     out_ref,
     normed, phased, halo_out, halo_in, lattice, near, far,
     dil, dil_other, combined, returned, win, win_other, rest,
+    w_ref, wout_ref, scores_a, scores_b, heads_out, load_sem,
     a2a_send, a2a_recv, halo_send, halo_recv, ret_send, ret_recv, pair_send, pair_recv,
 ):
     rows, cols, row_groups, col_groups = dims
@@ -222,6 +224,11 @@
     def place(p):
         return (branch, p // col_groups, p % col_groups)
 
+    w_copy = pltpu.make_async_copy(w_hbm, w_ref, load_sem.at[0])
+    w_copy.start()
+    wout_copy = pltpu.make_async_copy(wout_hbm, wout_ref, load_sem.at[1])
+    wout_copy.start()
+
     barrier = pltpu.get_barrier_semaphore()
 
     def greet(k, carry):
@@ -339,8 +346,6 @@
     piece = 2 * CHUNK
 
     def project_all(ref, load):
-        clear(ref, 0, tile, jnp.ones((1, 1), jnp.float32))
-
         def body(step, carry):
             part = step // (tile // piece)
             i = step % (tile // piece)
@@ -353,6 +358,9 @@
         lax.fori_loop(0, 3 * (tile // piece), body, 0)
 
     wide = piece // per
+    clear(near, 0, tile, jnp.ones((1, 1), jnp.float32))
+    clear(far, 0, tile, jnp.ones((1, 1), jnp.float32))
+    w_copy.wait()
     project_all(near, lambda i, at: phased[pl.ds(i * wide, wide)].reshape(piece, width))
 
     offset_at = pl.ds(pl.multiple_of(row * padded, padded), padded)
@@ -384,38 +392,53 @@
     lax.fori_loop(1, 3, project_halo, 0)
 
     def attend_heads(ref, first, last):
-        def body(h, carry):
-            keys = ref[HEADS + h]
+        keys = ref.shape[1]
+
+        def score(h, scores):
+            scores[:, 0:keys] = lax.dot_general(
+                ref[h, 0:tile, :], ref[HEADS + h], (((1,), (1,)), ((), ())),
+                preferred_element_type=jnp.float32,
+            )
+
+        def weigh(h, scores):
             values = ref[2 * HEADS + h]
-            for r in range(tile // CHUNK):
-                at = pl.ds(r * CHUNK, CHUNK)
-                scores = lax.dot_general(
-                    ref[h, at, :], keys, (((1,), (1,)), ((), ())),
-                    preferred_element_type=jnp.float32,
-                )
-                powers = jnp.exp2(scores - jnp.max(scores, axis=-1, keepdims=True))
+            for r in range(tile // piece):
+                at = pl.ds(r * piece, piece)
+                held = scores[at, 0:keys]
+                powers = jnp.exp2(held - jnp.max(held, axis=-1, keepdims=True))
                 got = jnp.dot(
                     powers.astype(jnp.bfloat16), values, preferred_element_type=jnp.float32
                 )
-                ref[h, at, :] = (got * (1.0 / got[:, size : size + 1])).astype(jnp.bfloat16)
+                got = got * (1.0 / got[:, size : size + 1])
+                heads_out[h, at, :] = got.astype(jnp.bfloat16)
+
+        score(first, scores_a)
+
+        def body(i, carry):
+            h = first + 2 * i
+            score(h + 1, scores_b)
+            weigh(h, scores_a)
+            score(jnp.minimum(h + 2, last - 1), scores_a)
+            weigh(h + 1, scores_b)
             return carry
 
-        lax.fori_loop(first, last, body, 0)
-
-    def gather_heads(ref, target):
+        lax.fori_loop(0, (last - first) // 2, body, 0)
+
+    def gather_heads(target, first, last):
         count = target.shape[0] * CHUNK // tile
 
         def body(i, carry):
             at = pl.ds(pl.multiple_of(i * CHUNK, CHUNK), CHUNK)
             to = pl.ds(i * count, count)
-            for h in range(HEADS):
-                value = ref[h, at, 0:size].reshape(count, 2, per // 2, size)
+            for h in range(first, last):
+                value = heads_out[h, at, 0:size].reshape(count, 2, per // 2, size)
                 target[to, :, :, h * size : (h + 1) * size] = value
             return carry
 
         lax.fori_loop(0, tile // CHUNK, body, 0)
 
     attend_heads(near, 0, HEADS // 2)
+    gather_heads(win, 0, HEADS // 2)
 
     def take_in(k, carry):
         inward(k).wait_recv()
@@ -424,7 +447,7 @@
     lax.fori_loop(1, groups, take_in, 0)
     project_all(far, lambda i, at: lattice[pl.ds(i * wide, wide)].reshape(piece, width))
     attend_heads(far, 0, HEADS)
-    gather_heads(far, dil)
+    gather_heads(dil, 0, HEADS)
     dil_copy = pair_copy(1, dil.at[:, other], dil_other)
     dil_copy.start()
     dil_copy.wait_recv()
@@ -462,7 +485,7 @@
     returned[me] = combined[me]
 
     attend_heads(near, HEADS // 2, HEADS)
-    gather_heads(near, win)
+    gather_heads(win, HEADS // 2, HEADS)
     win_copy = pair_copy(2, win.at[:, other], win_other)
     win_copy.start()
 
@@ -474,7 +497,15 @@
     win_copy.wait_recv()
     tokens_copy.wait_recv()
 
-    weight = blend_ref[pl.ds(pl.multiple_of(branch * half, half), half), :]
+    shares = blend_ref[pl.ds(pl.multiple_of(branch * (rows // 2), rows // 2), rows // 2), :]
+    r_at = offs_ref[2 * padded :, 0:1]
+    c_at = offs_ref[2 * padded :, 1:2]
+    weight = jnp.zeros((half, cols), jnp.float32)
+    for r in range(rows // 2):
+        weight = jnp.where(r_at == r, shares[r : r + 1, :], weight)
+    picked = c_at == lax.broadcasted_iota(jnp.int32, (half, cols), 1)
+    weight = jnp.sum(jnp.where(picked, weight, 0.0), axis=-1, keepdims=True)
+    wout_copy.wait()
     window = mine * win[:, branch].astype(jnp.float32) + theirs * win_other[...].astype(jnp.float32)
     window = window.reshape(half, width)
     dilated = returned[...].astype(jnp.float32).reshape(half, width)
@@ -510,14 +541,13 @@
     _, sent = halo_slots(rows, cols)
     padded = -(-(tile + sent) // LANES) * LANES - tile
     select, restore, offsets = selections(rows, cols, row_groups, col_groups, padded)
-    order = blend.reshape(2, rows // row_groups // 2, row_groups, cols // col_groups, col_groups)
-    order = order.transpose(0, 2, 4, 1, 3).reshape(tile, 1)
     bf16 = jnp.bfloat16
     vmem = pl.BlockSpec(memory_space=pltpu.VMEM)
     out = pl.pallas_call(
         functools.partial(fused, dims),
         out_shape=jax.ShapeDtypeStruct((half, width), bf16),
-        in_specs=[vmem] * 5 + [pl.BlockSpec(memory_space=pltpu.SMEM)] + [vmem] * 3,
+        in_specs=[vmem] * 2 + [pl.BlockSpec(memory_space=pl.ANY)] * 2 + [vmem]
+        + [pl.BlockSpec(memory_space=pltpu.SMEM)] + [vmem] * 3,
         out_specs=vmem,
         scratch_shapes=[
             pltpu.VMEM((tile, width), bf16),
@@ -534,6 +564,12 @@
             pltpu.VMEM((groups, 2, per // 2, width), bf16),
             pltpu.VMEM((groups, per // 2, width), bf16),
             pltpu.VMEM((half, width), bf16),
+            pltpu.VMEM(wqkv.shape, bf16),
+            pltpu.VMEM(w_out.shape, bf16),
+            pltpu.VMEM((tile, tile + padded), jnp.float32),
+            pltpu.VMEM((tile, tile + padded), jnp.float32),
+            pltpu.VMEM((HEADS, tile, LANES), bf16),
+            pltpu.SemaphoreType.DMA((2,)),
             pltpu.SemaphoreType.DMA((groups,)),
             pltpu.SemaphoreType.DMA((groups,)),
             pltpu.SemaphoreType.DMA((5,)),
@@ -547,7 +583,7 @@
             collective_id=0, has_side_effects=True, vmem_limit_bytes=60 * 1024 * 1024
         ),
     )(
-        tokens.reshape(tile, width), modulation, wqkv, w_out, order, reach.reshape(4),
+        tokens.reshape(tile, width), modulation, wqkv, w_out, blend, reach.reshape(4),
         jnp.asarray(select, bf16), jnp.asarray(restore, bf16), jnp.asarray(offsets),
     )
     return out.reshape(rows // 2, cols, width)
@@ -573,6 +609,7 @@
             and col_groups > 2
             and (rows * cols) % (32 * groups) == 0
             and rows // row_groups % 2 == 0
+            and rows % 16 == 0
         )
         body = on_device
         if fits:

time: 104 us -> 75.4 us (0.73)
  the two profiles are of different devices: /device:TPU:0 before, /device:TPU:24 now
where the time goes in v2:
time: 75.4 us; the launch traced here: 75.2 us
  Pallas kernels  73.2 us (97%)
  local copies, waits for them, and re-layouts  1.92 us (3%)
    pallas_call x1, Pallas kernels, on_device_fused(): pl.pallas_call(functools.partial(fused, dims), out_shape=jax.ShapeDtypeSt...  73.2 us
    unnamed x1, local copies, waits for them, and re-layouts  1.92 us

profile of v2, /device:TPU:24, one launch (start us, length us, event | category | flops | bytes accessed | tf_op | source)
XLA Modules:
  0.0 75.2 jit_solution(15173615876926736401)
XLA Ops:
  0.0 73.2 %shard_map.91 = bf16[256,1152]{1,0:T(8,128)(2,1)} custom-call(bf16[512,1152]{1,0:T(8,128)(2,1)} %bitcast.4, f32[3,1152]{1,0:T(4,128)} %mod_ref.1, bf16[1152,3456]{1,0:T(8,128)(2,1)} %w_hbm.1, bf16[1152,1152]{1,0:T(8,128)(2,1)} %wout_hbm.1, f32[16,32]{1,0:T(8,128)} %blend_ref.1, s32[4]{0:T(128)} %bitcast.5, bf16[1088,512]{1,0:T(8,128)(2,1)} %constant.6.clone.select_ref, ...), custom_call_target="tpu_custom_call" | custom-call | tf_op jit(solution)/shard_map/pallas_call | solution.py:546
  73.2 1.9 %copy.11 = bf16[8,32,1152]{2,1,0:T(8,128)(2,1)} copy(bf16[8,32,1152]{2,1,0:T(8,128)(2,1)} %bitcast.3) | data formatting | bytes 1179648
